TPU v7x, 128 devices: a whole 4x4x4 slice. The times are simulated.
128 devices in a mesh: grp: 4 (over x_lo, core), cond: 32 (over y, x_hi, z).
Axes of the slice: x: 4 (x_hi: 2, x_lo: 2; x = x_hi * 2 + x_lo), y: 4, z: 4, core: 2. Of those that a mesh axis runs over, the one named last changes fastest.
Arguments:
- valence_pairs: bfloat16 [64, 4096], P('grp', 'cond'), may hold values from -6 to 6
- screened: bfloat16 [4096, 4096], P('cond'), may hold values from -0.09375 to 0.09375
- cond_pairs: bfloat16 [262144, 4096], P(('grp', 'cond')), may hold values from -0.09375 to 0.09375
- owner_map: int32 [128, 32], P(('grp', 'cond')), may hold values from 0 to 31, as said below
- band_counts: int32 [128, 32], P(('grp', 'cond')), may hold values from 1 to 64, as said below
Outputs:
- owned_tiles: float32 [128, 32, 4096], P(('grp', 'cond'))
Inputs may be any that keep to these rules, and one draw needn't show every extreme that they name: `owner_map`: each row is a permutation of 0 .. 31. `band_counts`: each row holds the value 64 at least once.
All inputs are finite; a program needn't handle non-finite values.
Results may differ from a plain program's by a relative error of at most 0.0029.
Values may be sent and summed in bfloat16 or wider, within the bound.
No kernel may reach another device: no remote copies, remote signals or barrier semaphores. Data moves between devices by JAX's collectives and lax.ppermute only.
A program may use at most 64 MiB of HBM per device.

v0:
```python
import functools

import jax
import jax.numpy as jnp
from jax import lax
from jax.experimental import pallas as pl
from jax.experimental.pallas import tpu as pltpu
from jax.sharding import PartitionSpec as P

LANES = 128
CORES = 2
SPARE_ROWS = 8
VMEM = pl.BlockSpec(memory_space=pltpu.VMEM)
ANY = pl.BlockSpec(memory_space=pl.ANY)


def in_hbm(x):
    return pltpu.with_memory_space_constraint(x, pltpu.HBM)


def in_vmem(x):
    return pltpu.with_memory_space_constraint(x, pltpu.VMEM)


def exchanged(x, axes, groups=None):
    return lax.all_to_all(
        x, axes, split_axis=0, concat_axis=0, tiled=True, axis_index_groups=groups
    )


def from_other_core(x):
    count = lax.axis_size("grp")
    return lax.ppermute(x, "grp", [(i, i ^ 1) for i in range(count)])


def against(rows, other):
    return lax.dot_general(
        rows, other, (((1,), (1,)), ((), ())), preferred_element_type=jnp.float32
    )


def kernel_call(body, out_shape, in_specs, scratch=(), mib=16, flops=0, nbytes=0, out_space=VMEM, name=None):
    return pl.pallas_call(
        body,
        out_shape=out_shape,
        in_specs=in_specs,
        out_specs=jax.tree.map(lambda _: out_space, out_shape),
        scratch_shapes=scratch,
        compiler_params=pltpu.CompilerParams(vmem_limit_bytes=mib << 20),
        cost_estimate=pl.CostEstimate(flops=flops, bytes_accessed=nbytes, transcendentals=0),
        name=name,
    )


def core_half(own_half, width):
    core = lax.axis_index("grp") % CORES
    which = core if own_half else 1 - core
    return pl.ds(pl.multiple_of(which * width, width), width)


def load_body(valence_hbm, screened_hbm, valence_ref, screened_ref, sems):
    lanes = core_half(True, screened_ref.shape[1])
    copies = [
        pltpu.make_async_copy(screened_hbm.at[:, lanes], screened_ref, sems.at[0]),
        pltpu.make_async_copy(valence_hbm, valence_ref, sems.at[1]),
    ]
    for copy in copies:
        copy.start()
    for copy in copies:
        copy.wait()


def partial_body(own_ref, other_ref, screened_ref, out_ref):
    core = lax.axis_index("grp") % CORES
    half = screened_ref[...]
    rows = jnp.concatenate([own_ref[...], other_ref[...]], axis=0)
    both = jnp.dot(rows, half, preferred_element_type=jnp.float32)
    own, other = both[: own_ref.shape[0]], both[own_ref.shape[0] :]
    for t in range(half.shape[1] // LANES):
        lanes = slice(t * LANES, (t + 1) * LANES)
        out_ref[CORES * t + core] = own[:, lanes]
        out_ref[CORES * t + (1 - core)] = other[:, lanes]


def sum_body(pieces_ref, cond_ref, out_ref):
    total = pieces_ref[0]
    for c in range(1, pieces_ref.shape[0]):
        total = total + pieces_ref[c]
    rounded = total.astype(jnp.bfloat16)
    for d in range(out_ref.shape[0]):
        out_ref[d] = rounded


def half_of(own_half, cond_ref):
    return cond_ref[:, core_half(own_half, cond_ref.shape[1] // CORES)]


def assemble(groups, pieces_ref, projected):
    ncond = pieces_ref.shape[0] * CORES // groups
    rows_dev = pieces_ref.shape[1]
    valence_all = groups * rows_dev
    for d in range(pieces_ref.shape[0]):
        c = d % ncond
        group = CORES * (d // ncond) + c % CORES
        lanes = slice(c // CORES * LANES, (c // CORES + 1) * LANES)
        piece = pieces_ref[d]
        for start in (group * rows_dev, valence_all + group * rows_dev):
            projected[start : start + rows_dev, lanes] = piece


def first_body(groups, pieces_ref, cond_ref, out_ref, projected):
    assemble(groups, pieces_ref, projected)
    out_ref[...] = against(half_of(True, cond_ref), projected[...])


def tiles_body(
    groups, pieces_ref, cond_ref, first_ref, owner_ref, counts_ref, out_ref,
    projected, product, owner, counts, sems,
):
    loads = [
        pltpu.make_async_copy(owner_ref, owner, sems.at[0]),
        pltpu.make_async_copy(counts_ref, counts, sems.at[1]),
    ]
    for load in loads:
        load.start()
    assemble(groups, pieces_ref, projected)
    product[0 : first_ref.shape[0], :] = first_ref[...] + against(
        half_of(False, cond_ref), projected[...]
    )
    for load in loads:
        load.wait()
    ncond, pairs, _ = out_ref.shape
    tile_rows = 2 * pairs
    lane = lax.broadcasted_iota(jnp.int32, (pairs, LANES), 1)
    second = lane >= LANES // 2
    place = 2 * lax.broadcasted_iota(jnp.int32, (pairs, LANES), 0) + second.astype(jnp.int32)
    for j in range(ncond):
        even = product[pl.ds(tile_rows * j, pairs, stride=2), :]
        odd = product[pl.ds(tile_rows * j + 1, pairs, stride=2), :]
        tile = jnp.where(second, odd, even)
        tile = jnp.where(place < counts[0, j], tile, jnp.float32(0.0))
        out_ref[owner[0, j]] = tile.astype(jnp.bfloat16)


def widen_body(tiles_ref, out_ref, wide, sems):
    count, pairs, lanes = tiles_ref.shape
    copies = []
    for i in range(sems.shape[0]):
        rows = slice(i * count // sems.shape[0], (i + 1) * count // sems.shape[0])
        tiles = tiles_ref[rows].astype(jnp.float32)
        wide[rows, :] = tiles.reshape(tiles.shape[0], pairs * lanes)
        copies.append(
            pltpu.make_async_copy(wide.at[rows, :], out_ref.at[0, rows, :], sems.at[i])
        )
        copies[-1].start()
    for copy in copies:
        copy.wait()


def per_device(valence_pairs, screened, cond_pairs, owner_map, band_counts):
    groups = lax.axis_size("grp")
    ncond = lax.axis_size("cond")
    rows_dev = valence_pairs.shape[0]
    waves = screened.shape[1]
    pairs_dev = cond_pairs.shape[0]
    valence_all = groups * rows_dev
    tile_size = pairs_dev // ncond * valence_all
    pairs = tile_size // LANES
    same_core = [
        [g * ncond + c for g in range(core, groups, CORES) for c in range(ncond)]
        for core in range(CORES)
    ]

    own, screened_half = kernel_call(
        load_body,
        [
            pltpu.VMEM(valence_pairs.shape, valence_pairs.dtype),
            pltpu.VMEM((screened.shape[0], waves // CORES), screened.dtype),
        ],
        [ANY, ANY],
        scratch=[pltpu.SemaphoreType.DMA((2,))],
        nbytes=2 * screened.size,
        name="load_first",
    )(in_hbm(valence_pairs), in_hbm(screened))
    pieces = kernel_call(
        partial_body,
        jax.ShapeDtypeStruct((ncond, rows_dev, LANES), jnp.float32),
        [VMEM, VMEM, VMEM],
        flops=2 * rows_dev * screened.shape[0] * waves,
        nbytes=2 * screened.size,
        name="partial",
    )(
        in_vmem(own), from_other_core(valence_pairs), in_vmem(screened_half)
    )
    arrived = exchanged(pieces, "cond")
    copies = kernel_call(
        sum_body,
        jax.ShapeDtypeStruct((len(same_core[0]), rows_dev, LANES), jnp.bfloat16),
        [VMEM, ANY],
        nbytes=arrived.size * 4,
        name="sum_pieces",
    )(arrived, in_hbm(cond_pairs))
    gathered = exchanged(copies, ("grp", "cond"), same_core)
    others = from_other_core(gathered)
    half_scratch = [pltpu.VMEM((2 * valence_all, waves // CORES), jnp.bfloat16)]
    first = kernel_call(
        functools.partial(first_body, groups),
        jax.ShapeDtypeStruct((pairs_dev, LANES), jnp.float32),
        [VMEM, VMEM],
        scratch=half_scratch,
        flops=pairs_dev * waves * valence_all,
        nbytes=cond_pairs.size,
        name="first_half",
    )(gathered, cond_pairs)
    outgoing = kernel_call(
        functools.partial(tiles_body, groups),
        jax.ShapeDtypeStruct((ncond, pairs, LANES), jnp.bfloat16),
        [VMEM, VMEM, VMEM, ANY, ANY],
        scratch=[
            *half_scratch,
            pltpu.VMEM((pairs_dev + SPARE_ROWS, LANES), jnp.float32),
            pltpu.SMEM((1, ncond), jnp.int32),
            pltpu.SMEM((1, ncond), jnp.int32),
            pltpu.SemaphoreType.DMA((2,)),
        ],
        flops=pairs_dev * waves * valence_all,
        nbytes=cond_pairs.size,
        name="tiles",
    )(others, cond_pairs, first, in_hbm(owner_map), in_hbm(band_counts))
    tiles = exchanged(outgoing, "cond")
    return kernel_call(
        widen_body,
        jax.ShapeDtypeStruct((1, ncond, tile_size), jnp.float32),
        [VMEM],
        scratch=[
            pltpu.VMEM((ncond, tile_size), jnp.float32),
            pltpu.SemaphoreType.DMA((4,)),
        ],
        nbytes=6 * ncond * tile_size,
        out_space=ANY,
        name="widen",
    )(tiles)


def solution(mesh):
    return jax.shard_map(
        per_device,
        mesh=mesh,
        in_specs=(
            P("grp", "cond"),
            P("cond", None),
            P(("grp", "cond"), None),
            P(("grp", "cond"), None),
            P(("grp", "cond"), None),
        ),
        out_specs=P(("grp", "cond"), None, None),
        check_vma=False,
    )
```

profile of v0, /device:TPU:0, one launch (start us, length us, event | category | flops | bytes accessed | tf_op | source)
XLA Modules:
  0.0 59.5 jit_solution(18295999174442785702)
XLA Ops:
  0.0 0.0 copy-start
  0.0 0.0 collective-permute-start
  0.0 1.2 %load_first.1 = (bf16[16,128]{1,0:T(8,128)(2,1)S(1)}, bf16[128,2048]{1,0:T(8,128)(2,1)S(1)}) custom-call(bf16[16,128]{1,0:T(8,128)(2,1)} %valence_hbm.1, bf16[128,4096]{1,0:T(8,128)(2,1)} %screened_hbm.1), custom_call_target="tpu_custom_call" | custom-call | bytes 1048576 | tf_op jit(solution)/shard_map/load_first/pallas_call | solution.py:174
  1.2 0.2 collective-permute-done.other_ref
  1.4 0.2 partial.1
  1.6 22.2 %all_to_all.15.pieces_ref = f32[32,16,128]{2,1,0:T(8,128)S(1)} all-to-all(f32[32,16,128]{2,1,0:T(8,128)S(1)} %partial.1), channel_id=1, replica_groups=mesh['grp'=4,'cond'=32] {'cond'}, dimensions={0} | all-to-all | bytes 524288 | tf_op jit(solution)/shard_map/all_to_all | solution.py:26
  23.8 0.1 sum_pieces.1
  23.9 14.6 %all_to_all.16.pieces_ref = bf16[64,16,128]{2,1,0:T(8,128)(2,1)S(1)} all-to-all(bf16[64,16,128]{2,1,0:T(8,128)(2,1)S(1)} %sum_pieces.1), channel_id=1, replica_groups={{0,1,2,3,4,5,6,7,8,9,10,11,12,13,14,15,16,17,18,19,20,21,22,23,24,25,26..., dimensions={0} | all-to-all | bytes 524288 | tf_op jit(solution)/shard_map/all_to_all | solution.py:26
  38.5 0.0 collective-permute-start.1
  38.5 0.0 copy-done
  38.5 2.4 %first_half.1.first_ref = f32[2048,128]{1,0:T(8,128)S(1)} custom-call(bf16[64,16,128]{2,1,0:T(8,128)(2,1)S(1)} %all_to_all.16.pieces_ref, bf16[2048,4096]{1,0:T(8,128)(2,1)S(1)} %copy-done), custom_call_target="tpu_custom_call" | custom-call | flops 536870912 | bytes 8388608 | tf_op jit(solution)/shard_map/first_half/pallas_call | solution.py:206
  40.9 0.0 collective-permute-done.1.pieces_ref
  40.9 2.5 %tiles.1 = bf16[32,32,128]{2,1,0:T(8,128)(2,1)S(1)} custom-call(bf16[64,16,128]{2,1,0:T(8,128)(2,1)S(1)} %collective-permute-done.1.pieces_ref, bf16[2048,4096]{1,0:T(8,128)(2,1)S(1)} %copy-done, f32[2048,128]{1,0:T(8,128)S(1)} %first_half.1.first_ref, s32[1,32]{1,0:T(1,128)} %owner_ref.1, s32[1,32]{1,0:T(1,128)} %counts_ref.1), custom_call_target="tpu_custom_call" | custom-call | flops 536870912 | bytes 8388608 | tf_op jit(solution)/shard_map/tiles/pallas_call | solution.py:215
  43.4 15.2 %all_to_all.17.tiles_ref = bf16[32,32,128]{2,1,0:T(8,128)(2,1)S(1)} all-to-all(bf16[32,32,128]{2,1,0:T(8,128)(2,1)S(1)} %tiles.1), channel_id=1, replica_groups=mesh['grp'=4,'cond'=32] {'cond'}, dimensions={0} | all-to-all | bytes 524288 | tf_op jit(solution)/shard_map/all_to_all | solution.py:26
  58.7 0.8 %widen.1 = f32[1,32,4096]{2,1,0:T(8,128)} custom-call(bf16[32,32,128]{2,1,0:T(8,128)(2,1)S(1)} %all_to_all.17.tiles_ref), custom_call_target="tpu_custom_call" | custom-call | bytes 786432 | tf_op jit(solution)/shard_map/widen/pallas_call | solution.py:231
Async XLA Ops:
  0.0 38.5 %copy-start = (bf16[2048,4096]{1,0:T(8,128)(2,1)S(1)}, bf16[2048,4096]{1,0:T(8,128)(2,1)}, u32[]{:S(2)}) copy-start(bf16[2048,4096]{1,0:T(8,128)(2,1)} %cond_ref.5) | copy-start | bytes 50331652
  0.0 1.4 %collective-permute-start = (bf16[16,128]{1,0:T(8,128)(2,1)}, bf16[16,128]{1,0:T(8,128)(2,1)S(1)}, u32[]{:S(2)}, u32[]{:S(2)}) collective-permute-start(bf16[16,128]{1,0:T(8,128)(2,1)} %valence_hbm.1), channel_id=1, source_target_pairs={{0,32},{32,0},{64,96},{96,64},{1,33},{33,1},{65,97},{97,65},{2,34}... | collective-permute-start | bytes 12296 | tf_op jit(solution)/shard_map/ppermute | solution.py:33
  38.5 2.4 %collective-permute-start.1 = (bf16[64,16,128]{2,1,0:T(8,128)(2,1)S(1)}, bf16[64,16,128]{2,1,0:T(8,128)(2,1)S(1)}, u32[]{:S(2)}, u32[]{:S(2)}) collective-permute-start(bf16[64,16,128]{2,1,0:T(8,128)(2,1)S(1)} %all_to_all.16.pieces_ref), channel_id=1, source_target_pairs={{0,32},{32,0},{64,96},{96,64},{1,33},{33,1},{65,97},{97,65},{2,34}... | collective-permute-start | bytes 786440 | tf_op jit(solution)/shard_map/ppermute | solution.py:33
where the time goes:
time: 59.7 us; the launch traced here: 59.5 us
  blocking collectives  52.1 us (87%)
  Pallas kernels  7.2 us (12%)
    all_to_all x3, blocking collectives, exchanged(): lax.all_to_all(x, axes, split_axis=0, concat_axis=0, tiled=True, axis_ind...  52.1 us
    pallas_call x1, Pallas kernels, per_device(): kernel_call(functools.partial(tiles_body, groups), jax.ShapeDtypeStruct((...  2.49 us
    pallas_call x1, Pallas kernels, per_device(): kernel_call(functools.partial(first_body, groups), jax.ShapeDtypeStruct((...  2.39 us
    pallas_call x1, Pallas kernels, per_device(): kernel_call(load_body, [pltpu.VMEM(valence_pairs.shape, valence_pairs.dty...  1.21 us
  transfers between devices with their start and end apart: 2, of which 1 were waited for; matrix products, arithmetic and copies ran while one was open for 0% of the time, Pallas kernels for 6%

commit v1 on v0

--- a/solution.py
+++ b/solution.py
@@ -9,9 +9,11 @@
 
 LANES = 128
 CORES = 2
-SPARE_ROWS = 8
+BLOCK = 16
+EARLY, MAIN, FURTHER = 48, 104, (8, 16)
 VMEM = pl.BlockSpec(memory_space=pltpu.VMEM)
 ANY = pl.BlockSpec(memory_space=pl.ANY)
+SMEM = pl.BlockSpec(memory_space=pltpu.SMEM)
 
 
 def in_hbm(x):
@@ -44,7 +46,7 @@
         body,
         out_shape=out_shape,
         in_specs=in_specs,
-        out_specs=jax.tree.map(lambda _: out_space, out_shape),
+        out_specs=out_space,
         scratch_shapes=scratch,
         compiler_params=pltpu.CompilerParams(vmem_limit_bytes=mib << 20),
         cost_estimate=pl.CostEstimate(flops=flops, bytes_accessed=nbytes, transcendentals=0),
@@ -58,14 +60,34 @@
     return pl.ds(pl.multiple_of(which * width, width), width)
 
 
-def load_body(valence_hbm, screened_hbm, valence_ref, screened_ref, sems):
+def load_body(
+    valence_hbm, screened_hbm, counts_hbm, owner_hbm, valence_ref, screened_ref,
+    blocks_ref, bases_ref, counts, owner, sems,
+):
     lanes = core_half(True, screened_ref.shape[1])
+    first = pltpu.make_async_copy(counts_hbm, counts, sems.at[0])
     copies = [
-        pltpu.make_async_copy(screened_hbm.at[:, lanes], screened_ref, sems.at[0]),
-        pltpu.make_async_copy(valence_hbm, valence_ref, sems.at[1]),
+        pltpu.make_async_copy(screened_hbm.at[:, lanes], screened_ref, sems.at[1]),
+        pltpu.make_async_copy(valence_hbm, valence_ref, sems.at[2]),
+        pltpu.make_async_copy(owner_hbm, owner, sems.at[3]),
     ]
+    first.start()
     for copy in copies:
         copy.start()
+    ncond = counts.shape[1]
+    blocks = (MAIN + sum(FURTHER)) // ncond
+    for i in range(blocks_ref.shape[1]):
+        blocks_ref[0, i] = 0
+    first.wait()
+    used = jnp.int32(0)
+    for j in range(ncond):
+        bases_ref[0, j] = used
+        for i in range(blocks):
+            blocks_ref[0, used + i] = j * blocks + i
+        used = used + (counts[0, j] + (BLOCK - 1)) // BLOCK
+    for i in range(blocks):
+        blocks_ref[0, used + i] = 0
+    bases_ref[0, ncond] = used
     for copy in copies:
         copy.wait()
 
@@ -89,10 +111,6 @@
     rounded = total.astype(jnp.bfloat16)
     for d in range(out_ref.shape[0]):
         out_ref[d] = rounded
-
-
-def half_of(own_half, cond_ref):
-    return cond_ref[:, core_half(own_half, cond_ref.shape[1] // CORES)]
 
 
 def assemble(groups, pieces_ref, projected):
@@ -108,38 +126,76 @@
             projected[start : start + rows_dev, lanes] = piece
 
 
-def first_body(groups, pieces_ref, cond_ref, out_ref, projected):
+def rows_of(begin, end):
+    return slice(begin * BLOCK, end * BLOCK)
+
+
+def packed_product(begin, end, lanes, cond_ref, blocks_ref, projected):
+    rows = [
+        cond_ref[pl.ds(pl.multiple_of(blocks_ref[0, i] * BLOCK, BLOCK), BLOCK), lanes]
+        for i in range(begin, end)
+    ]
+    return against(jnp.concatenate(rows, axis=0), projected[...])
+
+
+def further_products(bases_ref, chunk):
+    used = bases_ref[0, bases_ref.shape[1] - 1]
+    begin = MAIN
+    for count in FURTHER:
+        pl.when(used > begin)(functools.partial(chunk, begin, begin + count))
+        begin += count
+
+
+def first_body(groups, pieces_ref, cond_ref, blocks_ref, bases_ref, out_ref, projected):
     assemble(groups, pieces_ref, projected)
-    out_ref[...] = against(half_of(True, cond_ref), projected[...])
+    lanes = core_half(True, projected.shape[1])
+
+    def chunk(begin, end):
+        out_ref[rows_of(begin, end), :] = packed_product(
+            begin, end, lanes, cond_ref, blocks_ref, projected
+        )
+
+    chunk(0, MAIN)
+    further_products(bases_ref, chunk)
 
 
 def tiles_body(
-    groups, pieces_ref, cond_ref, first_ref, owner_ref, counts_ref, out_ref,
-    projected, product, owner, counts, sems,
+    groups, pieces_ref, cond_ref, first_ref, blocks_ref, bases_ref, counts, owner,
+    out_ref, projected, early, total,
 ):
-    loads = [
-        pltpu.make_async_copy(owner_ref, owner, sems.at[0]),
-        pltpu.make_async_copy(counts_ref, counts, sems.at[1]),
-    ]
-    for load in loads:
-        load.start()
     assemble(groups, pieces_ref, projected)
-    product[0 : first_ref.shape[0], :] = first_ref[...] + against(
-        half_of(False, cond_ref), projected[...]
-    )
-    for load in loads:
-        load.wait()
+    lanes = core_half(False, projected.shape[1])
     ncond, pairs, _ = out_ref.shape
-    tile_rows = 2 * pairs
     lane = lax.broadcasted_iota(jnp.int32, (pairs, LANES), 1)
     second = lane >= LANES // 2
     place = 2 * lax.broadcasted_iota(jnp.int32, (pairs, LANES), 0) + second.astype(jnp.int32)
-    for j in range(ncond):
-        even = product[pl.ds(tile_rows * j, pairs, stride=2), :]
-        odd = product[pl.ds(tile_rows * j + 1, pairs, stride=2), :]
-        tile = jnp.where(second, odd, even)
-        tile = jnp.where(place < counts[0, j], tile, jnp.float32(0.0))
-        out_ref[owner[0, j]] = tile.astype(jnp.bfloat16)
+
+    def chunk(begin, end):
+        rows = rows_of(begin, end)
+        total[rows, :] = first_ref[rows, :] + packed_product(
+            begin, end, lanes, cond_ref, blocks_ref, projected
+        )
+
+    def put_tiles(source, tiles):
+        for j in tiles:
+            begin = pl.multiple_of(bases_ref[0, j] * BLOCK, BLOCK)
+            even = source[pl.ds(begin, pairs, stride=2), :]
+            odd = source[pl.ds(begin + 1, pairs, stride=2), :]
+            tile = jnp.where(second, odd, even)
+            tile = jnp.where(place < counts[0, j], tile, jnp.float32(0.0))
+            out_ref[owner[0, j]] = tile.astype(jnp.bfloat16)
+
+    rows = rows_of(0, EARLY)
+    product = first_ref[rows, :] + packed_product(
+        0, EARLY, lanes, cond_ref, blocks_ref, projected
+    )
+    early[rows, :] = product
+    total[rows, :] = product
+    chunk(EARLY, MAIN)
+    safe = EARLY // (2 * pairs // BLOCK)
+    put_tiles(early, range(safe))
+    further_products(bases_ref, chunk)
+    put_tiles(total, range(safe, ncond))
 
 
 def widen_body(tiles_ref, out_ref, wide, sems):
@@ -171,17 +227,23 @@
         for core in range(CORES)
     ]
 
-    own, screened_half = kernel_call(
+    tile_rows = pairs_dev // ncond
+    own, screened_half, blocks, bases, counts, owner = kernel_call(
         load_body,
         [
             pltpu.VMEM(valence_pairs.shape, valence_pairs.dtype),
             pltpu.VMEM((screened.shape[0], waves // CORES), screened.dtype),
+            pltpu.SMEM((1, pairs_dev // BLOCK + tile_rows // BLOCK), jnp.int32),
+            pltpu.SMEM((1, ncond + 1), jnp.int32),
+            pltpu.SMEM(band_counts.shape, band_counts.dtype),
+            pltpu.SMEM(owner_map.shape, owner_map.dtype),
         ],
-        [ANY, ANY],
-        scratch=[pltpu.SemaphoreType.DMA((2,))],
+        [ANY, ANY, ANY, ANY],
+        scratch=[pltpu.SemaphoreType.DMA((4,))],
         nbytes=2 * screened.size,
+        out_space=[VMEM, VMEM, SMEM, SMEM, SMEM, SMEM],
         name="load_first",
-    )(in_hbm(valence_pairs), in_hbm(screened))
+    )(in_hbm(valence_pairs), in_hbm(screened), in_hbm(band_counts), in_hbm(owner_map))
     pieces = kernel_call(
         partial_body,
         jax.ShapeDtypeStruct((ncond, rows_dev, LANES), jnp.float32),
@@ -206,27 +268,25 @@
     first = kernel_call(
         functools.partial(first_body, groups),
         jax.ShapeDtypeStruct((pairs_dev, LANES), jnp.float32),
-        [VMEM, VMEM],
+        [VMEM, VMEM, SMEM, SMEM],
         scratch=half_scratch,
         flops=pairs_dev * waves * valence_all,
         nbytes=cond_pairs.size,
         name="first_half",
-    )(gathered, cond_pairs)
+    )(gathered, cond_pairs, blocks, bases)
     outgoing = kernel_call(
         functools.partial(tiles_body, groups),
         jax.ShapeDtypeStruct((ncond, pairs, LANES), jnp.bfloat16),
-        [VMEM, VMEM, VMEM, ANY, ANY],
+        [VMEM, VMEM, VMEM, SMEM, SMEM, SMEM, SMEM],
         scratch=[
             *half_scratch,
-            pltpu.VMEM((pairs_dev + SPARE_ROWS, LANES), jnp.float32),
-            pltpu.SMEM((1, ncond), jnp.int32),
-            pltpu.SMEM((1, ncond), jnp.int32),
-            pltpu.SemaphoreType.DMA((2,)),
+            pltpu.VMEM((EARLY * BLOCK + tile_rows + BLOCK, LANES), jnp.float32),
+            pltpu.VMEM((pairs_dev + tile_rows + BLOCK, LANES), jnp.float32),
         ],
         flops=pairs_dev * waves * valence_all,
         nbytes=cond_pairs.size,
         name="tiles",
-    )(others, cond_pairs, first, in_hbm(owner_map), in_hbm(band_counts))
+    )(others, cond_pairs, first, blocks, bases, counts, owner)
     tiles = exchanged(outgoing, "cond")
     return kernel_call(
         widen_body,

time: 59.7 us -> 58.9 us (0.987)
  Pallas kernels: 7.2 us -> 6.37 us
  transfers between devices with their start and end apart: 2 -> 2, of which waited for: 1 -> 1; matrix products, arithmetic and copies ran while one was open for 0% -> 0% of each run, Pallas kernels for 6% -> 5%
where the time goes in v1:
time: 58.9 us; the launch traced here: 58.7 us
  blocking collectives  52.1 us (88%)
  Pallas kernels  6.37 us (11%)
    all_to_all x3, blocking collectives, exchanged(): lax.all_to_all(x, axes, split_axis=0, concat_axis=0, tiled=True, axis_ind...  52.1 us
    pallas_call x1, Pallas kernels, per_device(): kernel_call(functools.partial(tiles_body, groups), jax.ShapeDtypeStruct((...  2.05 us
    pallas_call x1, Pallas kernels, per_device(): kernel_call(functools.partial(first_body, groups), jax.ShapeDtypeStruct((...  1.98 us
    pallas_call x1, Pallas kernels, per_device(): kernel_call(load_body, [pltpu.VMEM(valence_pairs.shape, valence_pairs.dty...  1.24 us
  transfers between devices with their start and end apart: 2, of which 1 were waited for; matrix products, arithmetic and copies ran while one was open for 0% of the time, Pallas kernels for 5%

profile of v1, /device:TPU:0, one launch (start us, length us, event | category | flops | bytes accessed | tf_op | source)
XLA Modules:
  0.0 58.7 jit_solution(4501669158397791557)
XLA Ops:
  0.0 0.0 copy-start
  0.0 0.0 collective-permute-start
  0.0 1.2 %load_first.1 = (bf16[16,128]{1,0:T(8,128)(2,1)S(1)}, bf16[128,2048]{1,0:T(8,128)(2,1)S(1)}, s32[1,132]{1,0:T(1,128)S(4)}, s32[1,33]{1,0:T(1,128)S(4)}, s32[1,32]{1,0:T(1,128)S(4)}, /*index=5*/s32[1,32]{1,0:T(1,128)S(4)}) custom-call(bf16[16,128]{1,0:T(8,128)(2,1)} %valence_hbm.1, bf16[128,4096]{1,0:T(8,128)(2,1)} %screened_hbm.1, s32[1,32]{1,0:T(1,128)} %counts_hbm.1, ...), custom_call_target="tpu_custom_call" | custom-call | bytes 1048576 | tf_op jit(solution)/shard_map/load_first/pallas_call | solution.py:231
  1.3 0.1 collective-permute-done.other_ref
  1.4 0.2 partial.1
  1.6 22.3 %all_to_all.15.pieces_ref = f32[32,16,128]{2,1,0:T(8,128)S(1)} all-to-all(f32[32,16,128]{2,1,0:T(8,128)S(1)} %partial.1), channel_id=1, replica_groups=mesh['grp'=4,'cond'=32] {'cond'}, dimensions={0} | all-to-all | bytes 524288 | tf_op jit(solution)/shard_map/all_to_all | solution.py:28
  23.8 0.1 sum_pieces.1
  23.9 14.6 %all_to_all.16.pieces_ref = bf16[64,16,128]{2,1,0:T(8,128)(2,1)S(1)} all-to-all(bf16[64,16,128]{2,1,0:T(8,128)(2,1)S(1)} %sum_pieces.1), channel_id=1, replica_groups={{0,1,2,3,4,5,6,7,8,9,10,11,12,13,14,15,16,17,18,19,20,21,22,23,24,25,26..., dimensions={0} | all-to-all | bytes 524288 | tf_op jit(solution)/shard_map/all_to_all | solution.py:28
  38.5 0.0 collective-permute-start.1
  38.5 0.0 copy-done
  38.5 2.0 %first_half.1.first_ref = f32[2048,128]{1,0:T(8,128)S(1)} custom-call(bf16[64,16,128]{2,1,0:T(8,128)(2,1)S(1)} %all_to_all.16.pieces_ref, bf16[2048,4096]{1,0:T(8,128)(2,1)S(1)} %copy-done, s32[1,132]{1,0:T(1,128)S(4)} %get-tuple-element.13.blocks_ref, s32[1,33]{1,0:T(1,128)S(4)} %get-tuple-element.14.bases_ref), custom_call_target="tpu_custom_call" | custom-call | flops 536870912 | bytes 8388608 | tf_op jit(solution)/shard_map/first_half/pallas_call | solution.py:268
  40.5 0.0 collective-permute-done.1.pieces_ref
  40.5 2.0 %tiles.1 = bf16[32,32,128]{2,1,0:T(8,128)(2,1)S(1)} custom-call(bf16[64,16,128]{2,1,0:T(8,128)(2,1)S(1)} %collective-permute-done.1.pieces_ref, bf16[2048,4096]{1,0:T(8,128)(2,1)S(1)} %copy-done, f32[2048,128]{1,0:T(8,128)S(1)} %first_half.1.first_ref, s32[1,132]{1,0:T(1,128)S(4)} %get-tuple-element.13.blocks_ref, s32[1,33]{1,0:T(1,128)S(4)} %get-tuple-element.14.bases_ref, ...), custom_call_target="tpu_custom_call" | custom-call | flops 536870912 | bytes 8388608 | tf_op jit(solution)/shard_map/tiles/pallas_call | solution.py:277
  42.6 15.2 %all_to_all.17.tiles_ref = bf16[32,32,128]{2,1,0:T(8,128)(2,1)S(1)} all-to-all(bf16[32,32,128]{2,1,0:T(8,128)(2,1)S(1)} %tiles.1), channel_id=1, replica_groups=mesh['grp'=4,'cond'=32] {'cond'}, dimensions={0} | all-to-all | bytes 524288 | tf_op jit(solution)/shard_map/all_to_all | solution.py:28
  57.8 0.8 %widen.1 = f32[1,32,4096]{2,1,0:T(8,128)} custom-call(bf16[32,32,128]{2,1,0:T(8,128)(2,1)S(1)} %all_to_all.17.tiles_ref), custom_call_target="tpu_custom_call" | custom-call | bytes 786432 | tf_op jit(solution)/shard_map/widen/pallas_call | solution.py:291
Async XLA Ops:
  0.0 38.5 %copy-start = (bf16[2048,4096]{1,0:T(8,128)(2,1)S(1)}, bf16[2048,4096]{1,0:T(8,128)(2,1)}, u32[]{:S(2)}) copy-start(bf16[2048,4096]{1,0:T(8,128)(2,1)} %cond_ref.5) | copy-start | bytes 50331652
  0.0 1.4 %collective-permute-start = (bf16[16,128]{1,0:T(8,128)(2,1)}, bf16[16,128]{1,0:T(8,128)(2,1)S(1)}, u32[]{:S(2)}, u32[]{:S(2)}) collective-permute-start(bf16[16,128]{1,0:T(8,128)(2,1)} %valence_hbm.1), channel_id=1, source_target_pairs={{0,32},{32,0},{64,96},{96,64},{1,33},{33,1},{65,97},{97,65},{2,34}... | collective-permute-start | bytes 12296 | tf_op jit(solution)/shard_map/ppermute | solution.py:35
  38.5 2.0 %collective-permute-start.1 = (bf16[64,16,128]{2,1,0:T(8,128)(2,1)S(1)}, bf16[64,16,128]{2,1,0:T(8,128)(2,1)S(1)}, u32[]{:S(2)}, u32[]{:S(2)}) collective-permute-start(bf16[64,16,128]{2,1,0:T(8,128)(2,1)S(1)} %all_to_all.16.pieces_ref), channel_id=1, source_target_pairs={{0,32},{32,0},{64,96},{96,64},{1,33},{33,1},{65,97},{97,65},{2,34}... | collective-permute-start | bytes 786440 | tf_op jit(solution)/shard_map/ppermute | solution.py:35

commit v2 on v1

--- a/solution.py
+++ b/solution.py
@@ -146,7 +146,7 @@
         begin += count
 
 
-def first_body(groups, pieces_ref, cond_ref, blocks_ref, bases_ref, out_ref, projected):
+def first_product(groups, pieces_ref, cond_ref, blocks_ref, bases_ref, out_ref, projected):
     assemble(groups, pieces_ref, projected)
     lanes = core_half(True, projected.shape[1])
 
@@ -157,6 +157,24 @@
 
     chunk(0, MAIN)
     further_products(bases_ref, chunk)
+
+
+def early_body(groups, *refs):
+    @pl.when(lax.axis_index("grp") % CORES == 1)
+    def _():
+        first_product(groups, *refs)
+
+
+def first_body(groups, early_ref, pieces_ref, cond_ref, blocks_ref, bases_ref, out_ref, projected):
+    core = lax.axis_index("grp") % CORES
+
+    @pl.when(core == 1)
+    def _():
+        out_ref[...] = early_ref[...]
+
+    @pl.when(core == 0)
+    def _():
+        first_product(groups, pieces_ref, cond_ref, blocks_ref, bases_ref, out_ref, projected)
 
 
 def tiles_body(
@@ -263,17 +281,28 @@
         name="sum_pieces",
     )(arrived, in_hbm(cond_pairs))
     gathered = exchanged(copies, ("grp", "cond"), same_core)
-    others = from_other_core(gathered)
     half_scratch = [pltpu.VMEM((2 * valence_all, waves // CORES), jnp.bfloat16)]
-    first = kernel_call(
-        functools.partial(first_body, groups),
-        jax.ShapeDtypeStruct((pairs_dev, LANES), jnp.float32),
+    half_product = jax.ShapeDtypeStruct((pairs_dev, LANES), jnp.float32)
+    early = kernel_call(
+        functools.partial(early_body, groups),
+        half_product,
         [VMEM, VMEM, SMEM, SMEM],
         scratch=half_scratch,
         flops=pairs_dev * waves * valence_all,
         nbytes=cond_pairs.size,
-        name="first_half",
+        name="first_half_core1",
     )(gathered, cond_pairs, blocks, bases)
+    gathered, early = lax.optimization_barrier((gathered, early))
+    others = from_other_core(gathered)
+    first = kernel_call(
+        functools.partial(first_body, groups),
+        half_product,
+        [VMEM, VMEM, VMEM, SMEM, SMEM],
+        scratch=half_scratch,
+        flops=pairs_dev * waves * valence_all,
+        nbytes=cond_pairs.size,
+        name="first_half_core0",
+    )(early, gathered, cond_pairs, blocks, bases)
     outgoing = kernel_call(
         functools.partial(tiles_body, groups),
         jax.ShapeDtypeStruct((ncond, pairs, LANES), jnp.bfloat16),

time: 58.9 us -> 58.6 us (level)
    pallas_call x1 -> x2, Pallas kernels: 1.98 us -> 1.98 us  [the longest x1 1.98 us: per_device(): kernel_call(functools.partial(first_body, groups), half_product, [VMEM, V...]
  transfers between devices with their start and end apart: 2 -> 2, of which waited for: 1 -> 1; matrix products, arithmetic and copies ran while one was open for 0% -> 0% of each run, Pallas kernels for 5% -> 6%
where the time goes in v2:
time: 58.6 us; the launch traced here: 58.4 us
  blocking collectives  51.7 us (88%)
  Pallas kernels  6.37 us (11%)
    all_to_all x3, blocking collectives, exchanged(): lax.all_to_all(x, axes, split_axis=0, concat_axis=0, tiled=True, axis_ind...  51.7 us
    pallas_call x1, Pallas kernels, per_device(): kernel_call(functools.partial(tiles_body, groups), jax.ShapeDtypeStruct((...  2.05 us
    pallas_call x1, Pallas kernels, per_device(): kernel_call(functools.partial(first_body, groups), half_product, [VMEM, V...  1.98 us
    pallas_call x1, Pallas kernels, per_device(): kernel_call(load_body, [pltpu.VMEM(valence_pairs.shape, valence_pairs.dty...  1.24 us
  transfers between devices with their start and end apart: 2, of which 1 were waited for; matrix products, arithmetic and copies ran while one was open for 0% of the time, Pallas kernels for 6%

profile of v2, /device:TPU:0, one launch (start us, length us, event | category | flops | bytes accessed | tf_op | source)
XLA Modules:
  0.0 58.4 jit_solution(9684317778553028251)
XLA Ops:
  0.0 0.0 copy-start
  0.0 0.0 collective-permute-start
  0.0 1.2 %load_first.1 = (bf16[16,128]{1,0:T(8,128)(2,1)S(1)}, bf16[128,2048]{1,0:T(8,128)(2,1)S(1)}, s32[1,132]{1,0:T(1,128)S(4)}, s32[1,33]{1,0:T(1,128)S(4)}, s32[1,32]{1,0:T(1,128)S(4)}, /*index=5*/s32[1,32]{1,0:T(1,128)S(4)}) custom-call(bf16[16,128]{1,0:T(8,128)(2,1)} %valence_hbm.1, bf16[128,4096]{1,0:T(8,128)(2,1)} %screened_hbm.1, s32[1,32]{1,0:T(1,128)} %counts_hbm.1, ...), custom_call_target="tpu_custom_call" | custom-call | bytes 1048576 | tf_op jit(solution)/shard_map/load_first/pallas_call | solution.py:249
  1.3 0.1 collective-permute-done.other_ref
  1.4 0.2 partial.1
  1.6 22.3 %all_to_all.15.pieces_ref = f32[32,16,128]{2,1,0:T(8,128)S(1)} all-to-all(f32[32,16,128]{2,1,0:T(8,128)S(1)} %partial.1), channel_id=1, replica_groups=mesh['grp'=4,'cond'=32] {'cond'}, dimensions={0} | all-to-all | bytes 524288 | tf_op jit(solution)/shard_map/all_to_all | solution.py:28
  23.8 0.1 sum_pieces.1
  23.9 14.6 %all_to_all.16.refs_0_.pieces_ref = bf16[64,16,128]{2,1,0:T(8,128)(2,1)S(1)} all-to-all(bf16[64,16,128]{2,1,0:T(8,128)(2,1)S(1)} %sum_pieces.1), channel_id=1, replica_groups={{0,1,2,3,4,5,6,7,8,9,10,11,12,13,14,15,16,17,18,19,20,21,22,23,24,25,26..., dimensions={0} | all-to-all | bytes 524288 | tf_op jit(solution)/shard_map/all_to_all | solution.py:28
  38.5 0.0 copy-done
  38.5 0.1 collective-permute-start.1
  38.7 2.0 %first_half_core0.1.first_ref = f32[2048,128]{1,0:T(8,128)S(1)} custom-call(f32[2048,128]{1,0:T(8,128)S(1)} %first_half_core1.1.early_ref, bf16[64,16,128]{2,1,0:T(8,128)(2,1)S(1)} %all_to_all.16.refs_0_.pieces_ref, bf16[2048,4096]{1,0:T(8,128)(2,1)S(1)} %copy-done, s32[1,132]{1,0:T(1,128)S(4)} %get-tuple-element.15.refs_2_.blocks_ref, ...), custom_call_target="tpu_custom_call" | custom-call | flops 536870912 | bytes 8388608 | tf_op jit(solution)/shard_map/first_half_core0/pallas_call | solution.py:297
  40.6 0.0 collective-permute-done.1.pieces_ref
  40.7 2.1 %tiles.1 = bf16[32,32,128]{2,1,0:T(8,128)(2,1)S(1)} custom-call(bf16[64,16,128]{2,1,0:T(8,128)(2,1)S(1)} %collective-permute-done.1.pieces_ref, bf16[2048,4096]{1,0:T(8,128)(2,1)S(1)} %copy-done, f32[2048,128]{1,0:T(8,128)S(1)} %first_half_core0.1.first_ref, s32[1,132]{1,0:T(1,128)S(4)} %get-tuple-element.15.refs_2_.blocks_ref, ...), custom_call_target="tpu_custom_call" | custom-call | flops 536870912 | bytes 8388608 | tf_op jit(solution)/shard_map/tiles/pallas_call | solution.py:306
  42.7 14.8 %all_to_all.17.tiles_ref = bf16[32,32,128]{2,1,0:T(8,128)(2,1)S(1)} all-to-all(bf16[32,32,128]{2,1,0:T(8,128)(2,1)S(1)} %tiles.1), channel_id=1, replica_groups=mesh['grp'=4,'cond'=32] {'cond'}, dimensions={0} | all-to-all | bytes 524288 | tf_op jit(solution)/shard_map/all_to_all | solution.py:28
  57.6 0.8 %widen.1 = f32[1,32,4096]{2,1,0:T(8,128)} custom-call(bf16[32,32,128]{2,1,0:T(8,128)(2,1)S(1)} %all_to_all.17.tiles_ref), custom_call_target="tpu_custom_call" | custom-call | bytes 786432 | tf_op jit(solution)/shard_map/widen/pallas_call | solution.py:320
  (1 shorter events, 0.0 us)
Async XLA Ops:
  0.0 38.5 %copy-start = (bf16[2048,4096]{1,0:T(8,128)(2,1)S(1)}, bf16[2048,4096]{1,0:T(8,128)(2,1)}, u32[]{:S(2)}) copy-start(bf16[2048,4096]{1,0:T(8,128)(2,1)} %cond_ref.5) | copy-start | bytes 50331652
  0.0 1.4 %collective-permute-start = (bf16[16,128]{1,0:T(8,128)(2,1)}, bf16[16,128]{1,0:T(8,128)(2,1)S(1)}, u32[]{:S(2)}, u32[]{:S(2)}) collective-permute-start(bf16[16,128]{1,0:T(8,128)(2,1)} %valence_hbm.1), channel_id=1, source_target_pairs={{0,32},{32,0},{64,96},{96,64},{1,33},{33,1},{65,97},{97,65},{2,34}... | collective-permute-start | bytes 12296 | tf_op jit(solution)/shard_map/ppermute | solution.py:35
  38.5 2.1 %collective-permute-start.1 = (bf16[64,16,128]{2,1,0:T(8,128)(2,1)S(1)}, bf16[64,16,128]{2,1,0:T(8,128)(2,1)S(1)}, u32[]{:S(2)}, u32[]{:S(2)}) collective-permute-start(bf16[64,16,128]{2,1,0:T(8,128)(2,1)S(1)} %all_to_all.16.refs_0_.pieces_ref), channel_id=1, source_target_pairs={{0,32},{32,0},{64,96},{96,64},{1,33},{33,1},{65,97},{97,65},{2,34}... | collective-permute-start | bytes 786440 | tf_op jit(solution)/shard_map/ppermute | solution.py:35

commit v3 on v2

--- a/solution.py
+++ b/solution.py
@@ -9,6 +9,7 @@
 
 LANES = 128
 CORES = 2
+ROOT = 22
 BLOCK = 16
 EARLY, MAIN, FURTHER = 48, 104, (8, 16)
 VMEM = pl.BlockSpec(memory_space=pltpu.VMEM)
@@ -100,8 +101,9 @@
     own, other = both[: own_ref.shape[0]], both[own_ref.shape[0] :]
     for t in range(half.shape[1] // LANES):
         lanes = slice(t * LANES, (t + 1) * LANES)
-        out_ref[CORES * t + core] = own[:, lanes]
-        out_ref[CORES * t + (1 - core)] = other[:, lanes]
+        place = (CORES * t) ^ ROOT
+        out_ref[place + core] = own[:, lanes]
+        out_ref[place + (1 - core)] = other[:, lanes]
 
 
 def sum_body(pieces_ref, cond_ref, out_ref):
@@ -118,7 +120,7 @@
     rows_dev = pieces_ref.shape[1]
     valence_all = groups * rows_dev
     for d in range(pieces_ref.shape[0]):
-        c = d % ncond
+        c = (d % ncond) ^ ROOT
         group = CORES * (d // ncond) + c % CORES
         lanes = slice(c // CORES * LANES, (c // CORES + 1) * LANES)
         piece = pieces_ref[d]
@@ -201,7 +203,7 @@
             odd = source[pl.ds(begin + 1, pairs, stride=2), :]
             tile = jnp.where(second, odd, even)
             tile = jnp.where(place < counts[0, j], tile, jnp.float32(0.0))
-            out_ref[owner[0, j]] = tile.astype(jnp.bfloat16)
+            out_ref[owner[0, j] ^ ROOT] = tile.astype(jnp.bfloat16)
 
     rows = rows_of(0, EARLY)
     product = first_ref[rows, :] + packed_product(
@@ -221,7 +223,8 @@
     copies = []
     for i in range(sems.shape[0]):
         rows = slice(i * count // sems.shape[0], (i + 1) * count // sems.shape[0])
-        tiles = tiles_ref[rows].astype(jnp.float32)
+        order = [tiles_ref[s ^ ROOT] for s in range(rows.start, rows.stop)]
+        tiles = jnp.stack(order).astype(jnp.float32)
         wide[rows, :] = tiles.reshape(tiles.shape[0], pairs * lanes)
         copies.append(
             pltpu.make_async_copy(wide.at[rows, :], out_ref.at[0, rows, :], sems.at[i])
@@ -240,8 +243,10 @@
     valence_all = groups * rows_dev
     tile_size = pairs_dev // ncond * valence_all
     pairs = tile_size // LANES
+    order = [p ^ ROOT for p in range(ncond)]
+    same_grp = [[g * ncond + c for c in order] for g in range(groups)]
     same_core = [
-        [g * ncond + c for g in range(core, groups, CORES) for c in range(ncond)]
+        [g * ncond + c for g in range(core, groups, CORES) for c in order]
         for core in range(CORES)
     ]
 
@@ -272,7 +277,7 @@
     )(
         in_vmem(own), from_other_core(valence_pairs), in_vmem(screened_half)
     )
-    arrived = exchanged(pieces, "cond")
+    arrived = exchanged(pieces, ("grp", "cond"), same_grp)
     copies = kernel_call(
         sum_body,
         jax.ShapeDtypeStruct((len(same_core[0]), rows_dev, LANES), jnp.bfloat16),
@@ -316,7 +321,7 @@
         nbytes=cond_pairs.size,
         name="tiles",
     )(others, cond_pairs, first, blocks, bases, counts, owner)
-    tiles = exchanged(outgoing, "cond")
+    tiles = exchanged(outgoing, ("grp", "cond"), same_grp)
     return kernel_call(
         widen_body,
         jax.ShapeDtypeStruct((1, ncond, tile_size), jnp.float32),

time: 58.6 us -> 53.8 us (0.918)
  blocking collectives: 51.7 us -> 46.7 us
    all_to_all x3, blocking collectives: 51.7 us -> 46.7 us  [exchanged(): lax.all_to_all(x, axes, split_axis=0, concat_axis=0, tiled=True, axis_ind...]
where the time goes in v3:
time: 53.8 us; the launch traced here: 53.4 us
  blocking collectives  46.7 us (87%)
  Pallas kernels  6.37 us (12%)
    all_to_all x3, blocking collectives, exchanged(): lax.all_to_all(x, axes, split_axis=0, concat_axis=0, tiled=True, axis_ind...  46.7 us
    pallas_call x1, Pallas kernels, per_device(): kernel_call(functools.partial(tiles_body, groups), jax.ShapeDtypeStruct((...  2.05 us
    pallas_call x1, Pallas kernels, per_device(): kernel_call(functools.partial(first_body, groups), half_product, [VMEM, V...  1.98 us
    pallas_call x1, Pallas kernels, per_device(): kernel_call(load_body, [pltpu.VMEM(valence_pairs.shape, valence_pairs.dty...  1.24 us
  transfers between devices with their start and end apart: 2, of which 1 were waited for; matrix products, arithmetic and copies ran while one was open for 0% of the time, Pallas kernels for 6%

profile of v3, /device:TPU:0, one launch (start us, length us, event | category | flops | bytes accessed | tf_op | source)
XLA Modules:
  0.0 53.4 jit_solution(17361329524073851558)
XLA Ops:
  0.0 0.0 copy-start
  0.0 0.0 collective-permute-start
  0.0 1.2 %load_first.1 = (bf16[16,128]{1,0:T(8,128)(2,1)S(1)}, bf16[128,2048]{1,0:T(8,128)(2,1)S(1)}, s32[1,132]{1,0:T(1,128)S(4)}, s32[1,33]{1,0:T(1,128)S(4)}, s32[1,32]{1,0:T(1,128)S(4)}, /*index=5*/s32[1,32]{1,0:T(1,128)S(4)}) custom-call(bf16[16,128]{1,0:T(8,128)(2,1)} %valence_hbm.1, bf16[128,4096]{1,0:T(8,128)(2,1)} %screened_hbm.1, s32[1,32]{1,0:T(1,128)} %counts_hbm.1, ...), custom_call_target="tpu_custom_call" | custom-call | bytes 1048576 | tf_op jit(solution)/shard_map/load_first/pallas_call | solution.py:254
  1.3 0.1 collective-permute-done.other_ref
  1.4 0.2 partial.1
  1.6 17.2 %all_to_all.15.pieces_ref = f32[32,16,128]{2,1,0:T(8,128)S(1)} all-to-all(f32[32,16,128]{2,1,0:T(8,128)S(1)} %partial.1), channel_id=1, replica_groups={{22,23,20,21,18,19,16,17,30,31,28,29,26,27,24,25,6,7,4,5,2,3,0,1,14,15,..., dimensions={0} | all-to-all | bytes 524288 | tf_op jit(solution)/shard_map/all_to_all | solution.py:29
  18.8 0.1 sum_pieces.1
  18.8 15.5 %all_to_all.16.refs_0_.pieces_ref = bf16[64,16,128]{2,1,0:T(8,128)(2,1)S(1)} all-to-all(bf16[64,16,128]{2,1,0:T(8,128)(2,1)S(1)} %sum_pieces.1), channel_id=1, replica_groups={{22,23,20,21,18,19,16,17,30,31,28,29,26,27,24,25,6,7,4,5,2,3,0,1,14,15,..., dimensions={0} | all-to-all | bytes 524288 | tf_op jit(solution)/shard_map/all_to_all | solution.py:29
  34.3 0.0 copy-done
  34.3 0.2 collective-permute-start.1
  34.5 2.0 %first_half_core0.1.first_ref = f32[2048,128]{1,0:T(8,128)S(1)} custom-call(f32[2048,128]{1,0:T(8,128)S(1)} %first_half_core1.1.early_ref, bf16[64,16,128]{2,1,0:T(8,128)(2,1)S(1)} %all_to_all.16.refs_0_.pieces_ref, bf16[2048,4096]{1,0:T(8,128)(2,1)S(1)} %copy-done, s32[1,132]{1,0:T(1,128)S(4)} %get-tuple-element.15.refs_2_.blocks_ref, ...), custom_call_target="tpu_custom_call" | custom-call | flops 536870912 | bytes 8388608 | tf_op jit(solution)/shard_map/first_half_core0/pallas_call | solution.py:302
  36.5 0.0 collective-permute-done.1.pieces_ref
  36.5 2.0 %tiles.1 = bf16[32,32,128]{2,1,0:T(8,128)(2,1)S(1)} custom-call(bf16[64,16,128]{2,1,0:T(8,128)(2,1)S(1)} %collective-permute-done.1.pieces_ref, bf16[2048,4096]{1,0:T(8,128)(2,1)S(1)} %copy-done, f32[2048,128]{1,0:T(8,128)S(1)} %first_half_core0.1.first_ref, s32[1,132]{1,0:T(1,128)S(4)} %get-tuple-element.15.refs_2_.blocks_ref, ...), custom_call_target="tpu_custom_call" | custom-call | flops 536870912 | bytes 8388608 | tf_op jit(solution)/shard_map/tiles/pallas_call | solution.py:311
  38.6 14.0 %all_to_all.17.tiles_ref = bf16[32,32,128]{2,1,0:T(8,128)(2,1)S(1)} all-to-all(bf16[32,32,128]{2,1,0:T(8,128)(2,1)S(1)} %tiles.1), channel_id=1, replica_groups={{22,23,20,21,18,19,16,17,30,31,28,29,26,27,24,25,6,7,4,5,2,3,0,1,14,15,..., dimensions={0} | all-to-all | bytes 524288 | tf_op jit(solution)/shard_map/all_to_all | solution.py:29
  52.6 0.8 %widen.1 = f32[1,32,4096]{2,1,0:T(8,128)} custom-call(bf16[32,32,128]{2,1,0:T(8,128)(2,1)S(1)} %all_to_all.17.tiles_ref), custom_call_target="tpu_custom_call" | custom-call | bytes 786432 | tf_op jit(solution)/shard_map/widen/pallas_call | solution.py:325
  (1 shorter events, 0.0 us)
Async XLA Ops:
  0.0 34.3 %copy-start = (bf16[2048,4096]{1,0:T(8,128)(2,1)S(1)}, bf16[2048,4096]{1,0:T(8,128)(2,1)}, u32[]{:S(2)}) copy-start(bf16[2048,4096]{1,0:T(8,128)(2,1)} %cond_ref.5) | copy-start | bytes 50331652
  0.0 1.4 %collective-permute-start = (bf16[16,128]{1,0:T(8,128)(2,1)}, bf16[16,128]{1,0:T(8,128)(2,1)S(1)}, u32[]{:S(2)}, u32[]{:S(2)}) collective-permute-start(bf16[16,128]{1,0:T(8,128)(2,1)} %valence_hbm.1), channel_id=1, source_target_pairs={{0,32},{32,0},{64,96},{96,64},{1,33},{33,1},{65,97},{97,65},{2,34}... | collective-permute-start | bytes 12296 | tf_op jit(solution)/shard_map/ppermute | solution.py:36
  34.3 2.2 %collective-permute-start.1 = (bf16[64,16,128]{2,1,0:T(8,128)(2,1)S(1)}, bf16[64,16,128]{2,1,0:T(8,128)(2,1)S(1)}, u32[]{:S(2)}, u32[]{:S(2)}) collective-permute-start(bf16[64,16,128]{2,1,0:T(8,128)(2,1)S(1)} %all_to_all.16.refs_0_.pieces_ref), channel_id=1, source_target_pairs={{0,32},{32,0},{64,96},{96,64},{1,33},{33,1},{65,97},{97,65},{2,34}... | collective-permute-start | bytes 786440 | tf_op jit(solution)/shard_map/ppermute | solution.py:36

commit v4 on v3

--- a/solution.py
+++ b/solution.py
@@ -11,7 +11,7 @@
 CORES = 2
 ROOT = 22
 BLOCK = 16
-EARLY, MAIN, FURTHER = 48, 104, (8, 16)
+EARLY, MAIN, FURTHER = 48, 100, (4, 8, 16)
 VMEM = pl.BlockSpec(memory_space=pltpu.VMEM)
 ANY = pl.BlockSpec(memory_space=pl.ANY)
 SMEM = pl.BlockSpec(memory_space=pltpu.SMEM)

time: 53.8 us -> 53.6 us (level)
  no operation moved by 1% of the time
where the time goes in v4:
time: 53.6 us; the launch traced here: 53.2 us
  blocking collectives  46.7 us (87%)
  Pallas kernels  6.25 us (12%)
    all_to_all x3, blocking collectives, exchanged(): lax.all_to_all(x, axes, split_axis=0, concat_axis=0, tiled=True, axis_ind...  46.7 us
    pallas_call x1, Pallas kernels, per_device(): kernel_call(functools.partial(tiles_body, groups), jax.ShapeDtypeStruct((...  1.99 us
    pallas_call x1, Pallas kernels, per_device(): kernel_call(functools.partial(first_body, groups), half_product, [VMEM, V...  1.92 us
    pallas_call x1, Pallas kernels, per_device(): kernel_call(load_body, [pltpu.VMEM(valence_pairs.shape, valence_pairs.dty...  1.24 us
  transfers between devices with their start and end apart: 2, of which 1 were waited for; matrix products, arithmetic and copies ran while one was open for 0% of the time, Pallas kernels for 6%

profile of v4, /device:TPU:0, one launch (start us, length us, event | category | flops | bytes accessed | tf_op | source)
XLA Modules:
  0.0 53.2 jit_solution(3108063656586739358)
XLA Ops:
  0.0 0.0 copy-start
  0.0 0.0 collective-permute-start
  0.0 1.2 %load_first.1 = (bf16[16,128]{1,0:T(8,128)(2,1)S(1)}, bf16[128,2048]{1,0:T(8,128)(2,1)S(1)}, s32[1,132]{1,0:T(1,128)S(4)}, s32[1,33]{1,0:T(1,128)S(4)}, s32[1,32]{1,0:T(1,128)S(4)}, /*index=5*/s32[1,32]{1,0:T(1,128)S(4)}) custom-call(bf16[16,128]{1,0:T(8,128)(2,1)} %valence_hbm.1, bf16[128,4096]{1,0:T(8,128)(2,1)} %screened_hbm.1, s32[1,32]{1,0:T(1,128)} %counts_hbm.1, ...), custom_call_target="tpu_custom_call" | custom-call | bytes 1048576 | tf_op jit(solution)/shard_map/load_first/pallas_call | solution.py:254
  1.3 0.1 collective-permute-done.other_ref
  1.4 0.2 partial.1
  1.6 17.2 %all_to_all.15.pieces_ref = f32[32,16,128]{2,1,0:T(8,128)S(1)} all-to-all(f32[32,16,128]{2,1,0:T(8,128)S(1)} %partial.1), channel_id=1, replica_groups={{22,23,20,21,18,19,16,17,30,31,28,29,26,27,24,25,6,7,4,5,2,3,0,1,14,15,..., dimensions={0} | all-to-all | bytes 524288 | tf_op jit(solution)/shard_map/all_to_all | solution.py:29
  18.8 0.1 sum_pieces.1
  18.8 15.5 %all_to_all.16.refs_0_.pieces_ref = bf16[64,16,128]{2,1,0:T(8,128)(2,1)S(1)} all-to-all(bf16[64,16,128]{2,1,0:T(8,128)(2,1)S(1)} %sum_pieces.1), channel_id=1, replica_groups={{22,23,20,21,18,19,16,17,30,31,28,29,26,27,24,25,6,7,4,5,2,3,0,1,14,15,..., dimensions={0} | all-to-all | bytes 524288 | tf_op jit(solution)/shard_map/all_to_all | solution.py:29
  34.3 0.0 copy-done
  34.3 0.1 collective-permute-start.1
  34.4 1.9 %first_half_core0.1.first_ref = f32[2048,128]{1,0:T(8,128)S(1)} custom-call(f32[2048,128]{1,0:T(8,128)S(1)} %first_half_core1.1.early_ref, bf16[64,16,128]{2,1,0:T(8,128)(2,1)S(1)} %all_to_all.16.refs_0_.pieces_ref, bf16[2048,4096]{1,0:T(8,128)(2,1)S(1)} %copy-done, s32[1,132]{1,0:T(1,128)S(4)} %get-tuple-element.15.refs_2_.blocks_ref, ...), custom_call_target="tpu_custom_call" | custom-call | flops 536870912 | bytes 8388608 | tf_op jit(solution)/shard_map/first_half_core0/pallas_call | solution.py:302
  36.4 0.0 collective-permute-done.1.pieces_ref
  36.4 2.0 %tiles.1 = bf16[32,32,128]{2,1,0:T(8,128)(2,1)S(1)} custom-call(bf16[64,16,128]{2,1,0:T(8,128)(2,1)S(1)} %collective-permute-done.1.pieces_ref, bf16[2048,4096]{1,0:T(8,128)(2,1)S(1)} %copy-done, f32[2048,128]{1,0:T(8,128)S(1)} %first_half_core0.1.first_ref, s32[1,132]{1,0:T(1,128)S(4)} %get-tuple-element.15.refs_2_.blocks_ref, ...), custom_call_target="tpu_custom_call" | custom-call | flops 536870912 | bytes 8388608 | tf_op jit(solution)/shard_map/tiles/pallas_call | solution.py:311
  38.4 14.0 %all_to_all.17.tiles_ref = bf16[32,32,128]{2,1,0:T(8,128)(2,1)S(1)} all-to-all(bf16[32,32,128]{2,1,0:T(8,128)(2,1)S(1)} %tiles.1), channel_id=1, replica_groups={{22,23,20,21,18,19,16,17,30,31,28,29,26,27,24,25,6,7,4,5,2,3,0,1,14,15,..., dimensions={0} | all-to-all | bytes 524288 | tf_op jit(solution)/shard_map/all_to_all | solution.py:29
  52.4 0.8 %widen.1 = f32[1,32,4096]{2,1,0:T(8,128)} custom-call(bf16[32,32,128]{2,1,0:T(8,128)(2,1)S(1)} %all_to_all.17.tiles_ref), custom_call_target="tpu_custom_call" | custom-call | bytes 786432 | tf_op jit(solution)/shard_map/widen/pallas_call | solution.py:325
  (1 shorter events, 0.0 us)
Async XLA Ops:
  0.0 34.3 %copy-start = (bf16[2048,4096]{1,0:T(8,128)(2,1)S(1)}, bf16[2048,4096]{1,0:T(8,128)(2,1)}, u32[]{:S(2)}) copy-start(bf16[2048,4096]{1,0:T(8,128)(2,1)} %cond_ref.5) | copy-start | bytes 50331652
  0.0 1.4 %collective-permute-start = (bf16[16,128]{1,0:T(8,128)(2,1)}, bf16[16,128]{1,0:T(8,128)(2,1)S(1)}, u32[]{:S(2)}, u32[]{:S(2)}) collective-permute-start(bf16[16,128]{1,0:T(8,128)(2,1)} %valence_hbm.1), channel_id=1, source_target_pairs={{0,32},{32,0},{64,96},{96,64},{1,33},{33,1},{65,97},{97,65},{2,34}... | collective-permute-start | bytes 12296 | tf_op jit(solution)/shard_map/ppermute | solution.py:36
  34.3 2.1 %collective-permute-start.1 = (bf16[64,16,128]{2,1,0:T(8,128)(2,1)S(1)}, bf16[64,16,128]{2,1,0:T(8,128)(2,1)S(1)}, u32[]{:S(2)}, u32[]{:S(2)}) collective-permute-start(bf16[64,16,128]{2,1,0:T(8,128)(2,1)S(1)} %all_to_all.16.refs_0_.pieces_ref), channel_id=1, source_target_pairs={{0,32},{32,0},{64,96},{96,64},{1,33},{33,1},{65,97},{97,65},{2,34}... | collective-permute-start | bytes 786440 | tf_op jit(solution)/shard_map/ppermute | solution.py:36
